TPU v7x, 512 devices: a whole 4x4x16 slice. The times are simulated.
512 devices in a mesh: blk: 128 (over x_lo, z, y), pair: 4 (over x_hi, core).
Axes of the slice: x: 4 (x_hi: 2, x_lo: 2; x = x_hi * 2 + x_lo), y: 4, z: 16, core: 2. Of those that a mesh axis runs over, the one named last changes fastest.
Arguments:
- series: bfloat16 [1024, 4096], P(None, 'blk'), may hold values from -2000 to 2000
- assign: int32 [1024], replicated, may hold values from 0 to 1023, each once
Outputs:
- cross: float32 [128, 4, 16, 8, 8, 256], P('blk', 'pair')
- opposite: float32 [128, 8, 8, 256], P('blk', None, None, 'pair')
Inputs may be any that keep to these rules, and one draw needn't show every extreme that they name: `assign`: a permutation of the 1024 probe ids.
All inputs are finite; a program needn't handle non-finite values.
Results may differ from a plain program's by a relative error of at most 0.0041.
Values may be sent and summed in bfloat16 or wider, within the bound.
A program may use at most 128 MiB of HBM per device.

v0:
```python
import math

import jax
import jax.numpy as jnp
from jax import lax
from jax.sharding import PartitionSpec as P

BINS = 1024
HALF_LAG = 128


def shifted(block, axis, distance):
    devices = range(lax.axis_size(axis))
    route = [((i - distance) % len(devices), i) for i in devices]
    return lax.ppermute(block, axis, route)


def spectra_table(samples, bin_count):
    time_index = jnp.arange(samples, dtype=jnp.int32)
    frequencies = jnp.arange(1, bin_count + 1, dtype=jnp.int32)
    phases = time_index[:, None] * frequencies[None, :] % samples
    angles = phases.astype(jnp.float32) * jnp.float32(2.0 * math.pi / samples)
    norm_scale = 1.0 / math.sqrt(samples)
    table_whole = jnp.stack([jnp.cos(angles) * norm_scale, jnp.sin(angles) * norm_scale], axis=1)
    return table_whole.astype(jnp.bfloat16)


def spectra_part(series_rows, table_part):
    bin_count = table_part.shape[2]
    flat_table = table_part.reshape(table_part.shape[0], 2 * bin_count)
    running = jnp.dot(series_rows, flat_table, preferred_element_type=jnp.float32)
    return running.reshape(series_rows.shape[0], 2, bin_count)


def normalize(spectrum):
    energy = jnp.sum(spectrum * spectrum, axis=(1, 2))
    return (spectrum * lax.rsqrt(energy + 1e-06)[:, None, None]).astype(jnp.bfloat16)


def lags_table(bin_count, samples):
    frequencies = jnp.arange(1, bin_count + 1, dtype=jnp.int32)
    shifts = jnp.arange(2 * HALF_LAG, dtype=jnp.int32) - HALF_LAG + samples
    phases = frequencies[:, None] * shifts[None, :] % samples
    angles = phases.astype(jnp.float32) * jnp.float32(2.0 * math.pi / samples)
    lag_parts = jnp.stack([jnp.cos(angles), -jnp.sin(angles)], axis=0)
    return lag_parts.astype(jnp.bfloat16).reshape(2 * bin_count, 2 * HALF_LAG)


def pair_corr(left_unit, right_unit, lag_table):
    members = left_unit.shape[0]
    bin_count = left_unit.shape[2]
    left_wide = left_unit.astype(jnp.float32)
    right_wide = right_unit.astype(jnp.float32)
    real_part = (
        left_wide[:, None, 0, :] * right_wide[None, :, 0, :]
        + left_wide[:, None, 1, :] * right_wide[None, :, 1, :]
    )
    imag_part = (
        left_wide[:, None, 1, :] * right_wide[None, :, 0, :]
        - left_wide[:, None, 0, :] * right_wide[None, :, 1, :]
    )
    cross_spec = jnp.stack([real_part, imag_part], axis=2).astype(jnp.bfloat16)
    cross_spec = cross_spec.reshape(members * members, 2 * bin_count)
    result = jnp.dot(cross_spec, lag_table, preferred_element_type=jnp.float32)
    return result.reshape(members, members, lag_table.shape[1])


def body(series, assign):
    blocks = lax.axis_size("blk")
    groups = lax.axis_size("pair")
    my_lane = lax.axis_index("pair")
    per_group = blocks // (2 * groups)
    members = assign.shape[0] // blocks
    samples = series.shape[1] * blocks
    bin_count = BINS
    partner_offsets = jnp.reshape(my_lane * per_group, (1,))
    shared_offsets = jnp.array([0, blocks // 2], dtype=jnp.int32)
    offsets = jnp.concatenate([partner_offsets, shared_offsets])
    slot_count = offsets.shape[0]
    partner_count = partner_offsets.shape[0]
    targets = jnp.arange(blocks, dtype=jnp.int32)
    wanted = (targets[None, :] + offsets[:, None]) % blocks
    probe_ids = assign.reshape(blocks, members)[wanted]
    probe_ids = jnp.transpose(probe_ids, (0, 2, 1))
    outgoing = series[probe_ids].reshape(slot_count, members, blocks * series.shape[1])
    arrived = lax.all_to_all(outgoing, "blk", split_axis=2, concat_axis=2, tiled=True)
    raw_rows = arrived.reshape(slot_count * members, samples)
    split_row = partner_count * members
    table_all = spectra_table(samples, bin_count)
    unit_rows = normalize(spectra_part(raw_rows, table_all))
    partner_unit = unit_rows[:split_row]
    shared_unit = unit_rows[split_row:]
    own_unit = shared_unit[:members]
    far_unit = shared_unit[members:]
    lag_table = lags_table(bin_count, samples)
    lane_lags = lag_table.shape[1] // groups
    lag_slice = lax.dynamic_slice_in_dim(lag_table, my_lane * lane_lags, lane_lags, 1)
    opposite_out = pair_corr(own_unit, far_unit, lag_slice)[None]
    partner_unit = partner_unit.reshape(partner_count, members, 2, bin_count)

    def advance(current, unused):
        following = shifted(current, "blk", -1)
        return (following, pair_corr(own_unit, current, lag_table))

    first_unit = partner_unit[0]
    last_unit, earlier = lax.scan(advance, first_unit, None, length=per_group - 1)
    rounds = jnp.concatenate([earlier, pair_corr(own_unit, last_unit, lag_table)[None]], axis=0)
    cross_out = rounds[None, None]
    return (cross_out, opposite_out)


def solution(mesh):
    in_specs = (P(None, "blk"), P())
    out_specs = (P("blk", "pair", None, None, None, None), P("blk", None, None, "pair"))
    return jax.shard_map(body, mesh=mesh, in_specs=in_specs, out_specs=out_specs, check_vma=False)
```

profile of v0, /device:TPU:4, one launch (start us, length us, event | category | flops | bytes accessed | tf_op | source)
XLA Modules:
  0.0 293.5 jit_solution(3731209395663041849)
XLA Ops:
  3.8 9.2 %gather_fusion.1 = bf16[3072,32]{1,0:T(8,128)(2,1)S(1)} fusion(bf16[1024,32]{1,0:T(8,128)(2,1)S(1)} %copy.11, s32[3072]{0:T(1024)S(1)} %fusion.23), kind=kCustom, calls=%fused_computation.1 | custom fusion | bytes 405504 | tf_op jit(solution)/shard_map/gather | solution.py:85
  18.4 7.3 %reshape.465 = bf16[128,2,384]{2,1,0:T(2,128)(2,1)} reshape(bf16[4096,3,8]{2,1,0:T(4,128)(2,1)} %bitcast.90) | data formatting | bytes 393216
  25.7 20.6 %all-to-all-start = ((bf16[128,2,384]{2,1,0:T(2,128)(2,1)}), bf16[128,2,384]{2,1,0:T(2,128)(2,1)S(1)}, u32[]{:S(2)}, u32[]{:S(2)}) async-start(bf16[128,2,384]{2,1,0:T(2,128)(2,1)} %reshape.465), calls=%async_computation | async-start | bytes 393216 | tf_op jit(solution)/shard_map/all_to_all | solution.py:86
  46.3 70.5 %multiply_convert_fusion.1 = (bf16[4096,1,1024]{0,2,1:T(8,128)(2,1)}, bf16[4096,1,1024]{0,2,1:T(8,128)(2,1)}) fusion(s32[1024]{0:T(1024)S(1)} %iota_add_fusion), kind=kLoop, calls=%fused_computation.23 | loop fusion | flops 75497472 | bytes 16781312 | tf_op jit(solution)/shard_map/convert.6
  116.8 4.7 %fusion.17 = (bf16[1,1024,256]{2,1,0:T(8,128)(2,1)S(1)}, bf16[1,1024,256]{2,1,0:T(8,128)(2,1)S(1)}) fusion(s32[256]{0:T(256)S(1)} %iota_add_fusion.1, s32[1024]{0:T(1024)S(1)} %iota_add_fusion), kind=kLoop, calls=%fused_computation.43 | loop fusion | flops 4456448 | bytes 1053696 | tf_op jit(solution)/shard_map/cos | solution.py:45
  121.7 5.6 %reshape.466 = bf16[4096,3,8]{2,1,0:T(4,128)(2,1)} reshape(bf16[128,2,384]{2,1,0:T(2,128)(2,1)S(1)} %all-to-all-done) | data formatting | bytes 393216
  127.2 5.3 %copy.13 = bf16[3,8,4096]{2,1,0:T(8,128)(2,1)S(1)} copy(bf16[3,8,4096]{1,0,2:T(4,128)(2,1)} %bitcast.91) | data formatting | bytes 393216 | tf_op jit(solution)/shard_map/all_to_all | solution.py:86
  132.6 8.3 %multiply_reduce_fusion = (f32[24]{0:T(128)S(1)}, f32[24,2,1024]{2,0,1:T(8,128)S(1)}) fusion(bf16[4096,1,1024]{0,2,1:T(8,128)(2,1)} %get-tuple-element.67, bf16[4096,1,1024]{0,2,1:T(8,128)(2,1)} %get-tuple-element.66, bf16[3,8,4096]{2,1,0:T(8,128)(2,1)S(1)} %copy.13), kind=kOutput, calls=%fused_computation.54 | convolution fusion | flops 436305888 | bytes 17170528 | tf_op jit(solution)/shard_map/dot_general | solution.py:31
  141.0 150.0 %while.12 = (s32[]{:T(128)}, bf16[8,2,1024]{2,0,1:T(8,128)(2,1)S(1)}, f32[15,8,8,256]{3,2,1,0:T(8,128)S(1)}, bf16[8,2,1024]{2,0,1:T(8,128)(2,1)S(1)}, bf16[2048,256]{1,0:T(8,128)(2,1)S(1)}, /*index=5*/s32[]{:T(128)}) while((s32[]{:T(128)}, bf16[8,2,1024]{2,0,1:T(8,128)(2,1)S(1)}, f32[15,8,8,256]{3,2,1,0:T(8,128)S(1)}, ...), condition=%wide.region_2.3_spmd, body=%wide.region_1.2_spmd.sunk | while | flops 67796992 | bytes 2949233 | solution.py:106
  141.0 8.0 %collective-permute-start = (bf16[8,2,1024]{2,0,1:T(8,128)(2,1)S(1)}, bf16[8,2,1024]{2,0,1:T(8,128)(2,1)S(1)}, u32[]{:S(2)}, u32[]{:S(2)}) collective-permute-start(bf16[8,2,1024]{2,0,1:T(8,128)(2,1)S(1)} %copy.22), channel_id=1, source_target_pairs={{4,0},{8,4},{12,8},{16,12},{20,16},{24,20},{28,24},{32,28},{36,32}... | collective-permute-start | bytes 98312 | tf_op jit(solution)/shard_map/while/body/eval_jaxpr/ppermute | solution.py:15
  150.6 8.4 %collective-permute-start = (bf16[8,2,1024]{2,0,1:T(8,128)(2,1)S(1)}, bf16[8,2,1024]{2,0,1:T(8,128)(2,1)S(1)}, u32[]{:S(2)}, u32[]{:S(2)}) collective-permute-start(bf16[8,2,1024]{2,0,1:T(8,128)(2,1)S(1)} %copy.22), channel_id=1, source_target_pairs={{4,0},{8,4},{12,8},{16,12},{20,16},{24,20},{28,24},{32,28},{36,32}... | collective-permute-start | bytes 98312 | tf_op jit(solution)/shard_map/while/body/eval_jaxpr/ppermute | solution.py:15
  160.6 8.4 %collective-permute-start = (bf16[8,2,1024]{2,0,1:T(8,128)(2,1)S(1)}, bf16[8,2,1024]{2,0,1:T(8,128)(2,1)S(1)}, u32[]{:S(2)}, u32[]{:S(2)}) collective-permute-start(bf16[8,2,1024]{2,0,1:T(8,128)(2,1)S(1)} %copy.22), channel_id=1, source_target_pairs={{4,0},{8,4},{12,8},{16,12},{20,16},{24,20},{28,24},{32,28},{36,32}... | collective-permute-start | bytes 98312 | tf_op jit(solution)/shard_map/while/body/eval_jaxpr/ppermute | solution.py:15
  170.6 8.4 %collective-permute-start = (bf16[8,2,1024]{2,0,1:T(8,128)(2,1)S(1)}, bf16[8,2,1024]{2,0,1:T(8,128)(2,1)S(1)}, u32[]{:S(2)}, u32[]{:S(2)}) collective-permute-start(bf16[8,2,1024]{2,0,1:T(8,128)(2,1)S(1)} %copy.22), channel_id=1, source_target_pairs={{4,0},{8,4},{12,8},{16,12},{20,16},{24,20},{28,24},{32,28},{36,32}... | collective-permute-start | bytes 98312 | tf_op jit(solution)/shard_map/while/body/eval_jaxpr/ppermute | solution.py:15
  180.6 8.4 %collective-permute-start = (bf16[8,2,1024]{2,0,1:T(8,128)(2,1)S(1)}, bf16[8,2,1024]{2,0,1:T(8,128)(2,1)S(1)}, u32[]{:S(2)}, u32[]{:S(2)}) collective-permute-start(bf16[8,2,1024]{2,0,1:T(8,128)(2,1)S(1)} %copy.22), channel_id=1, source_target_pairs={{4,0},{8,4},{12,8},{16,12},{20,16},{24,20},{28,24},{32,28},{36,32}... | collective-permute-start | bytes 98312 | tf_op jit(solution)/shard_map/while/body/eval_jaxpr/ppermute | solution.py:15
  190.7 8.4 %collective-permute-start = (bf16[8,2,1024]{2,0,1:T(8,128)(2,1)S(1)}, bf16[8,2,1024]{2,0,1:T(8,128)(2,1)S(1)}, u32[]{:S(2)}, u32[]{:S(2)}) collective-permute-start(bf16[8,2,1024]{2,0,1:T(8,128)(2,1)S(1)} %copy.22), channel_id=1, source_target_pairs={{4,0},{8,4},{12,8},{16,12},{20,16},{24,20},{28,24},{32,28},{36,32}... | collective-permute-start | bytes 98312 | tf_op jit(solution)/shard_map/while/body/eval_jaxpr/ppermute | solution.py:15
  200.7 8.4 %collective-permute-start = (bf16[8,2,1024]{2,0,1:T(8,128)(2,1)S(1)}, bf16[8,2,1024]{2,0,1:T(8,128)(2,1)S(1)}, u32[]{:S(2)}, u32[]{:S(2)}) collective-permute-start(bf16[8,2,1024]{2,0,1:T(8,128)(2,1)S(1)} %copy.22), channel_id=1, source_target_pairs={{4,0},{8,4},{12,8},{16,12},{20,16},{24,20},{28,24},{32,28},{36,32}... | collective-permute-start | bytes 98312 | tf_op jit(solution)/shard_map/while/body/eval_jaxpr/ppermute | solution.py:15
  210.7 8.5 %collective-permute-start = (bf16[8,2,1024]{2,0,1:T(8,128)(2,1)S(1)}, bf16[8,2,1024]{2,0,1:T(8,128)(2,1)S(1)}, u32[]{:S(2)}, u32[]{:S(2)}) collective-permute-start(bf16[8,2,1024]{2,0,1:T(8,128)(2,1)S(1)} %copy.22), channel_id=1, source_target_pairs={{4,0},{8,4},{12,8},{16,12},{20,16},{24,20},{28,24},{32,28},{36,32}... | collective-permute-start | bytes 98312 | tf_op jit(solution)/shard_map/while/body/eval_jaxpr/ppermute | solution.py:15
  220.8 8.4 %collective-permute-start = (bf16[8,2,1024]{2,0,1:T(8,128)(2,1)S(1)}, bf16[8,2,1024]{2,0,1:T(8,128)(2,1)S(1)}, u32[]{:S(2)}, u32[]{:S(2)}) collective-permute-start(bf16[8,2,1024]{2,0,1:T(8,128)(2,1)S(1)} %copy.22), channel_id=1, source_target_pairs={{4,0},{8,4},{12,8},{16,12},{20,16},{24,20},{28,24},{32,28},{36,32}... | collective-permute-start | bytes 98312 | tf_op jit(solution)/shard_map/while/body/eval_jaxpr/ppermute | solution.py:15
  230.8 8.4 %collective-permute-start = (bf16[8,2,1024]{2,0,1:T(8,128)(2,1)S(1)}, bf16[8,2,1024]{2,0,1:T(8,128)(2,1)S(1)}, u32[]{:S(2)}, u32[]{:S(2)}) collective-permute-start(bf16[8,2,1024]{2,0,1:T(8,128)(2,1)S(1)} %copy.22), channel_id=1, source_target_pairs={{4,0},{8,4},{12,8},{16,12},{20,16},{24,20},{28,24},{32,28},{36,32}... | collective-permute-start | bytes 98312 | tf_op jit(solution)/shard_map/while/body/eval_jaxpr/ppermute | solution.py:15
  240.8 8.4 %collective-permute-start = (bf16[8,2,1024]{2,0,1:T(8,128)(2,1)S(1)}, bf16[8,2,1024]{2,0,1:T(8,128)(2,1)S(1)}, u32[]{:S(2)}, u32[]{:S(2)}) collective-permute-start(bf16[8,2,1024]{2,0,1:T(8,128)(2,1)S(1)} %copy.22), channel_id=1, source_target_pairs={{4,0},{8,4},{12,8},{16,12},{20,16},{24,20},{28,24},{32,28},{36,32}... | collective-permute-start | bytes 98312 | tf_op jit(solution)/shard_map/while/body/eval_jaxpr/ppermute | solution.py:15
  250.8 8.4 %collective-permute-start = (bf16[8,2,1024]{2,0,1:T(8,128)(2,1)S(1)}, bf16[8,2,1024]{2,0,1:T(8,128)(2,1)S(1)}, u32[]{:S(2)}, u32[]{:S(2)}) collective-permute-start(bf16[8,2,1024]{2,0,1:T(8,128)(2,1)S(1)} %copy.22), channel_id=1, source_target_pairs={{4,0},{8,4},{12,8},{16,12},{20,16},{24,20},{28,24},{32,28},{36,32}... | collective-permute-start | bytes 98312 | tf_op jit(solution)/shard_map/while/body/eval_jaxpr/ppermute | solution.py:15
  260.9 8.4 %collective-permute-start = (bf16[8,2,1024]{2,0,1:T(8,128)(2,1)S(1)}, bf16[8,2,1024]{2,0,1:T(8,128)(2,1)S(1)}, u32[]{:S(2)}, u32[]{:S(2)}) collective-permute-start(bf16[8,2,1024]{2,0,1:T(8,128)(2,1)S(1)} %copy.22), channel_id=1, source_target_pairs={{4,0},{8,4},{12,8},{16,12},{20,16},{24,20},{28,24},{32,28},{36,32}... | collective-permute-start | bytes 98312 | tf_op jit(solution)/shard_map/while/body/eval_jaxpr/ppermute | solution.py:15
  270.9 8.4 %collective-permute-start = (bf16[8,2,1024]{2,0,1:T(8,128)(2,1)S(1)}, bf16[8,2,1024]{2,0,1:T(8,128)(2,1)S(1)}, u32[]{:S(2)}, u32[]{:S(2)}) collective-permute-start(bf16[8,2,1024]{2,0,1:T(8,128)(2,1)S(1)} %copy.22), channel_id=1, source_target_pairs={{4,0},{8,4},{12,8},{16,12},{20,16},{24,20},{28,24},{32,28},{36,32}... | collective-permute-start | bytes 98312 | tf_op jit(solution)/shard_map/while/body/eval_jaxpr/ppermute | solution.py:15
  280.9 8.4 %collective-permute-start = (bf16[8,2,1024]{2,0,1:T(8,128)(2,1)S(1)}, bf16[8,2,1024]{2,0,1:T(8,128)(2,1)S(1)}, u32[]{:S(2)}, u32[]{:S(2)}) collective-permute-start(bf16[8,2,1024]{2,0,1:T(8,128)(2,1)S(1)} %copy.22), channel_id=1, source_target_pairs={{4,0},{8,4},{12,8},{16,12},{20,16},{24,20},{28,24},{32,28},{36,32}... | collective-permute-start | bytes 98312 | tf_op jit(solution)/shard_map/while/body/eval_jaxpr/ppermute | solution.py:15
  (162 shorter events, 34.1 us)
Async XLA Ops:
  25.7 95.9 %all-to-all-start = ((bf16[128,2,384]{2,1,0:T(2,128)(2,1)}), bf16[128,2,384]{2,1,0:T(2,128)(2,1)S(1)}, u32[]{:S(2)}, u32[]{:S(2)}) async-start(bf16[128,2,384]{2,1,0:T(2,128)(2,1)} %reshape.465), calls=%async_computation | async-start | bytes 393216 | tf_op jit(solution)/shard_map/all_to_all | solution.py:86
  141.0 9.6 %collective-permute-start = (bf16[8,2,1024]{2,0,1:T(8,128)(2,1)S(1)}, bf16[8,2,1024]{2,0,1:T(8,128)(2,1)S(1)}, u32[]{:S(2)}, u32[]{:S(2)}) collective-permute-start(bf16[8,2,1024]{2,0,1:T(8,128)(2,1)S(1)} %copy.22), channel_id=1, source_target_pairs={{4,0},{8,4},{12,8},{16,12},{20,16},{24,20},{28,24},{32,28},{36,32}... | collective-permute-start | bytes 98312 | tf_op jit(solution)/shard_map/while/body/eval_jaxpr/ppermute | solution.py:15
  150.6 10.0 %collective-permute-start = (bf16[8,2,1024]{2,0,1:T(8,128)(2,1)S(1)}, bf16[8,2,1024]{2,0,1:T(8,128)(2,1)S(1)}, u32[]{:S(2)}, u32[]{:S(2)}) collective-permute-start(bf16[8,2,1024]{2,0,1:T(8,128)(2,1)S(1)} %copy.22), channel_id=1, source_target_pairs={{4,0},{8,4},{12,8},{16,12},{20,16},{24,20},{28,24},{32,28},{36,32}... | collective-permute-start | bytes 98312 | tf_op jit(solution)/shard_map/while/body/eval_jaxpr/ppermute | solution.py:15
  160.6 10.0 %collective-permute-start = (bf16[8,2,1024]{2,0,1:T(8,128)(2,1)S(1)}, bf16[8,2,1024]{2,0,1:T(8,128)(2,1)S(1)}, u32[]{:S(2)}, u32[]{:S(2)}) collective-permute-start(bf16[8,2,1024]{2,0,1:T(8,128)(2,1)S(1)} %copy.22), channel_id=1, source_target_pairs={{4,0},{8,4},{12,8},{16,12},{20,16},{24,20},{28,24},{32,28},{36,32}... | collective-permute-start | bytes 98312 | tf_op jit(solution)/shard_map/while/body/eval_jaxpr/ppermute | solution.py:15
  170.6 10.0 %collective-permute-start = (bf16[8,2,1024]{2,0,1:T(8,128)(2,1)S(1)}, bf16[8,2,1024]{2,0,1:T(8,128)(2,1)S(1)}, u32[]{:S(2)}, u32[]{:S(2)}) collective-permute-start(bf16[8,2,1024]{2,0,1:T(8,128)(2,1)S(1)} %copy.22), channel_id=1, source_target_pairs={{4,0},{8,4},{12,8},{16,12},{20,16},{24,20},{28,24},{32,28},{36,32}... | collective-permute-start | bytes 98312 | tf_op jit(solution)/shard_map/while/body/eval_jaxpr/ppermute | solution.py:15
  180.6 10.0 %collective-permute-start = (bf16[8,2,1024]{2,0,1:T(8,128)(2,1)S(1)}, bf16[8,2,1024]{2,0,1:T(8,128)(2,1)S(1)}, u32[]{:S(2)}, u32[]{:S(2)}) collective-permute-start(bf16[8,2,1024]{2,0,1:T(8,128)(2,1)S(1)} %copy.22), channel_id=1, source_target_pairs={{4,0},{8,4},{12,8},{16,12},{20,16},{24,20},{28,24},{32,28},{36,32}... | collective-permute-start | bytes 98312 | tf_op jit(solution)/shard_map/while/body/eval_jaxpr/ppermute | solution.py:15
  190.7 10.0 %collective-permute-start = (bf16[8,2,1024]{2,0,1:T(8,128)(2,1)S(1)}, bf16[8,2,1024]{2,0,1:T(8,128)(2,1)S(1)}, u32[]{:S(2)}, u32[]{:S(2)}) collective-permute-start(bf16[8,2,1024]{2,0,1:T(8,128)(2,1)S(1)} %copy.22), channel_id=1, source_target_pairs={{4,0},{8,4},{12,8},{16,12},{20,16},{24,20},{28,24},{32,28},{36,32}... | collective-permute-start | bytes 98312 | tf_op jit(solution)/shard_map/while/body/eval_jaxpr/ppermute | solution.py:15
  200.7 10.0 %collective-permute-start = (bf16[8,2,1024]{2,0,1:T(8,128)(2,1)S(1)}, bf16[8,2,1024]{2,0,1:T(8,128)(2,1)S(1)}, u32[]{:S(2)}, u32[]{:S(2)}) collective-permute-start(bf16[8,2,1024]{2,0,1:T(8,128)(2,1)S(1)} %copy.22), channel_id=1, source_target_pairs={{4,0},{8,4},{12,8},{16,12},{20,16},{24,20},{28,24},{32,28},{36,32}... | collective-permute-start | bytes 98312 | tf_op jit(solution)/shard_map/while/body/eval_jaxpr/ppermute | solution.py:15
  210.7 10.1 %collective-permute-start = (bf16[8,2,1024]{2,0,1:T(8,128)(2,1)S(1)}, bf16[8,2,1024]{2,0,1:T(8,128)(2,1)S(1)}, u32[]{:S(2)}, u32[]{:S(2)}) collective-permute-start(bf16[8,2,1024]{2,0,1:T(8,128)(2,1)S(1)} %copy.22), channel_id=1, source_target_pairs={{4,0},{8,4},{12,8},{16,12},{20,16},{24,20},{28,24},{32,28},{36,32}... | collective-permute-start | bytes 98312 | tf_op jit(solution)/shard_map/while/body/eval_jaxpr/ppermute | solution.py:15
  220.8 10.0 %collective-permute-start = (bf16[8,2,1024]{2,0,1:T(8,128)(2,1)S(1)}, bf16[8,2,1024]{2,0,1:T(8,128)(2,1)S(1)}, u32[]{:S(2)}, u32[]{:S(2)}) collective-permute-start(bf16[8,2,1024]{2,0,1:T(8,128)(2,1)S(1)} %copy.22), channel_id=1, source_target_pairs={{4,0},{8,4},{12,8},{16,12},{20,16},{24,20},{28,24},{32,28},{36,32}... | collective-permute-start | bytes 98312 | tf_op jit(solution)/shard_map/while/body/eval_jaxpr/ppermute | solution.py:15
  230.8 10.0 %collective-permute-start = (bf16[8,2,1024]{2,0,1:T(8,128)(2,1)S(1)}, bf16[8,2,1024]{2,0,1:T(8,128)(2,1)S(1)}, u32[]{:S(2)}, u32[]{:S(2)}) collective-permute-start(bf16[8,2,1024]{2,0,1:T(8,128)(2,1)S(1)} %copy.22), channel_id=1, source_target_pairs={{4,0},{8,4},{12,8},{16,12},{20,16},{24,20},{28,24},{32,28},{36,32}... | collective-permute-start | bytes 98312 | tf_op jit(solution)/shard_map/while/body/eval_jaxpr/ppermute | solution.py:15
  240.8 10.0 %collective-permute-start = (bf16[8,2,1024]{2,0,1:T(8,128)(2,1)S(1)}, bf16[8,2,1024]{2,0,1:T(8,128)(2,1)S(1)}, u32[]{:S(2)}, u32[]{:S(2)}) collective-permute-start(bf16[8,2,1024]{2,0,1:T(8,128)(2,1)S(1)} %copy.22), channel_id=1, source_target_pairs={{4,0},{8,4},{12,8},{16,12},{20,16},{24,20},{28,24},{32,28},{36,32}... | collective-permute-start | bytes 98312 | tf_op jit(solution)/shard_map/while/body/eval_jaxpr/ppermute | solution.py:15
  250.8 10.0 %collective-permute-start = (bf16[8,2,1024]{2,0,1:T(8,128)(2,1)S(1)}, bf16[8,2,1024]{2,0,1:T(8,128)(2,1)S(1)}, u32[]{:S(2)}, u32[]{:S(2)}) collective-permute-start(bf16[8,2,1024]{2,0,1:T(8,128)(2,1)S(1)} %copy.22), channel_id=1, source_target_pairs={{4,0},{8,4},{12,8},{16,12},{20,16},{24,20},{28,24},{32,28},{36,32}... | collective-permute-start | bytes 98312 | tf_op jit(solution)/shard_map/while/body/eval_jaxpr/ppermute | solution.py:15
  260.9 10.0 %collective-permute-start = (bf16[8,2,1024]{2,0,1:T(8,128)(2,1)S(1)}, bf16[8,2,1024]{2,0,1:T(8,128)(2,1)S(1)}, u32[]{:S(2)}, u32[]{:S(2)}) collective-permute-start(bf16[8,2,1024]{2,0,1:T(8,128)(2,1)S(1)} %copy.22), channel_id=1, source_target_pairs={{4,0},{8,4},{12,8},{16,12},{20,16},{24,20},{28,24},{32,28},{36,32}... | collective-permute-start | bytes 98312 | tf_op jit(solution)/shard_map/while/body/eval_jaxpr/ppermute | solution.py:15
  270.9 10.0 %collective-permute-start = (bf16[8,2,1024]{2,0,1:T(8,128)(2,1)S(1)}, bf16[8,2,1024]{2,0,1:T(8,128)(2,1)S(1)}, u32[]{:S(2)}, u32[]{:S(2)}) collective-permute-start(bf16[8,2,1024]{2,0,1:T(8,128)(2,1)S(1)} %copy.22), channel_id=1, source_target_pairs={{4,0},{8,4},{12,8},{16,12},{20,16},{24,20},{28,24},{32,28},{36,32}... | collective-permute-start | bytes 98312 | tf_op jit(solution)/shard_map/while/body/eval_jaxpr/ppermute | solution.py:15
  280.9 10.0 %collective-permute-start = (bf16[8,2,1024]{2,0,1:T(8,128)(2,1)S(1)}, bf16[8,2,1024]{2,0,1:T(8,128)(2,1)S(1)}, u32[]{:S(2)}, u32[]{:S(2)}) collective-permute-start(bf16[8,2,1024]{2,0,1:T(8,128)(2,1)S(1)} %copy.22), channel_id=1, source_target_pairs={{4,0},{8,4},{12,8},{16,12},{20,16},{24,20},{28,24},{32,28},{36,32}... | collective-permute-start | bytes 98312 | tf_op jit(solution)/shard_map/while/body/eval_jaxpr/ppermute | solution.py:15
where the time goes:
time: 294 us; the launch traced here: 293 us
  starting transfers between devices  147 us (50%)
  other arithmetic  78.4 us (27%)
  local copies, waits for them, and re-layouts  36 us (12%)
  waiting for transfers between devices  16.5 us (6%)
  matrix products  13.9 us (5%)
    ppermute x15, starting transfers between devices, shifted(): return lax.ppermute(block, axis, route)  126 us
    another operation x18, other arithmetic  71.6 us
    all_to_all x1, starting transfers between devices, body(): lax.all_to_all(outgoing, 'blk', split_axis=2, concat_axis=2, tiled=True)  20.6 us
    ppermute x15, waiting for transfers between devices, shifted(): return lax.ppermute(block, axis, route)  16.5 us
    unnamed x3, local copies, waits for them, and re-layouts  14 us
    gather x1, local copies, waits for them, and re-layouts, body(): series[probe_ids].reshape(slot_count, members, blocks * series.shape[1])  9.16 us
    dot_general x1, matrix products, spectra_part(): jnp.dot(series_rows, flat_table, preferred_element_type=jnp.float32)  8.26 us
  transfers between devices with their start and end apart: 16, of which 15 were waited for; matrix products, arithmetic and copies ran while one was open for 28% of the time, Pallas kernels for 0%

commit v1 on v0

v1 whole, which is shorter than its diff:
```python
import math

import jax
import jax.numpy as jnp
import ml_dtypes
import numpy as np
from jax import lax
from jax.experimental import pallas as pl
from jax.experimental.pallas import tpu as pltpu
from jax.sharding import PartitionSpec as P

F32 = jnp.float32
BF16 = jnp.bfloat16
MESH = pl.DeviceIdType.MESH
N = 4096
OWN, OPP = 16, 17


def two_parts(x):
    high = x.astype(ml_dtypes.bfloat16)
    low = (x - high.astype(np.float64)).astype(ml_dtypes.bfloat16)
    return np.stack([high, low])


def tables():
    k1 = np.arange(32)
    z, h = np.arange(16), np.arange(2)
    n1 = 16 * h[None, :] + z[:, None]
    angle = 2 * np.pi * ((k1[:, None, None] + 1) * n1[None] % 32) / 32
    first = np.stack([np.cos(angle), np.sin(angle)]) / math.sqrt(N)
    first = np.einsum("ckzh,pr->ckpzhr", first, np.eye(8)).reshape(512, 256)
    n2 = np.arange(128)
    angle = 2 * np.pi * ((k1[:, None] + 1) * n2[None] % N) / N
    twiddle = np.stack([np.cos(angle), np.sin(angle)])
    twiddle = np.repeat(twiddle, 8, axis=1).astype(np.float32)
    k2 = np.arange(32)
    angle = 2 * np.pi * (n2[:, None] * k2[None] % 128) / 128
    co, si = np.cos(angle), np.sin(angle)
    second = np.array([[co, si], [-si, co]])
    second = np.einsum("rcnk,ab->arncbk", second, np.eye(4)).reshape(1024, 256)
    k1b, k1a = np.arange(8), np.arange(4)
    k = 1 + 8 * k1a[None, :, None] + k1b[:, None, None] + 32 * k2[None, None, :]
    shift = np.arange(256) - 128
    angle = 2 * np.pi * (k.reshape(1024)[:, None] * shift[None] % N) / N
    lag = np.concatenate([np.cos(angle), -np.sin(angle)]).astype(ml_dtypes.bfloat16)
    return two_parts(first), twiddle, two_parts(second), lag


def kernel(
    series, assign, first_hbm, twiddle_hbm, second_hbm, lag_hbm,
    cross, opposite,
    first, twiddle, second, lag, send1, recv1, send2, recv2, units, wide, lhs,
    load_sem, send1_sem, recv1_sem, send2_sem, recv2_sem, sendu_sem, recvu_sem, sende_sem,
):
    me, q = lax.axis_index("blk"), lax.axis_index("pair")
    half, z, y = me // 64, me // 4 % 16, me % 4
    spot = half * 4 + y

    def device(blk, pair=None):
        return {"blk": blk, "pair": q if pair is None else pair}

    def peer1(s):
        return s // 4 * 64 + z * 4 + s % 4

    def peer2(zz):
        return half * 64 + zz * 4 + y

    barrier = pltpu.get_barrier_semaphore()

    def greet(blk, pair=None):
        pl.semaphore_signal(barrier, 1, device_id=device(blk, pair), device_id_type=MESH)

    low_pair = q < 2
    edge = jnp.where(low_pair, 0, 3)
    own_from = jnp.where(low_pair, me + 120, me + 72) % 128
    opp_from = jnp.where(low_pair, me + 56, me + 8) % 128
    for d in range(1, 8):
        greet(peer1((spot + d) % 8))
    for d in range(1, 16):
        greet(peer2((z + d) % 16))
    for m in range(16):
        if m != 8:
            greet((me + m + 120) % 128)
    greet(own_from, edge)
    greet(opp_from, edge)

    loads = [
        pltpu.make_async_copy(src, dst, load_sem.at[i])
        for i, (src, dst) in enumerate(
            [(first_hbm, first), (twiddle_hbm, twiddle), (second_hbm, second), (lag_hbm, lag)]
        )
    ]
    for c in loads:
        c.start()

    ids = assign[...]
    turned = pltpu.roll(ids, 64, 1)
    rows = [turned] + [pltpu.roll(turned, 8 - k, 0) for k in range(1, 5)]

    def pick(first_row):
        out = rows[first_row + 3]
        for k in (2, 1, 0):
            out = jnp.where(q == k, rows[first_row + k], out)
        return out

    lane = lax.broadcasted_iota(jnp.int32, (8, 128), 1)
    row = lax.broadcasted_iota(jnp.int32, (8, 128), 0)
    moved = jnp.where(lane < 64, pick(0), pick(1))
    wanted = {}
    for yy in range(4):
        index = lane // 8 % 4 * 32 + yy * 8 + lane % 8
        got = jnp.take_along_axis(moved, index, axis=1)
        got = jnp.where(lane // 32 == row % 4, got, 0)
        for hh in range(2):
            wanted[hh * 4 + yy] = jnp.sum(got[hh * 4 : hh * 4 + 4], axis=0, keepdims=True)

    probe = lax.broadcasted_iota(jnp.int32, (1024, 256), 0)
    for s in range(0, 8, 2):
        pair_ids = jnp.concatenate([wanted[s], wanted[s + 1]], axis=1)
        hot = jnp.where(probe == pair_ids, 1.0, 0.0).astype(BF16)
        part = jnp.dot(series[...], hot, preferred_element_type=F32).astype(BF16)
        send1[s] = part[:, :128]
        send1[s + 1] = part[:, 128:]

    pl.semaphore_wait(barrier, 7 + 15 + 15 + jnp.where(jnp.logical_or(q == 0, q == 3), 4, 0))

    def remote(src, dst, ssem, rsem, blk, pair=None):
        return pltpu.make_async_remote_copy(
            src_ref=src, dst_ref=dst, send_sem=ssem, recv_sem=rsem,
            device_id=device(blk, pair), device_id_type=MESH,
        )

    stage1 = []
    for d in range(1, 8):
        s = (spot + d) % 8
        stage1.append(remote(send1.at[s], recv1.at[spot], send1_sem.at[d], recv1_sem.at[d], peer1(s)))
        stage1[-1].start()
    recv1[spot] = send1[spot]
    for c in stage1:
        c.wait_recv()
    sides = []
    for hh in range(2):
        side = recv1[hh * 4 : hh * 4 + 4].reshape(128, 128).astype(F32)
        sides.append(jnp.transpose(side).reshape(16, 8, 128))
    send2[...] = jnp.concatenate(sides, axis=1).astype(BF16)

    stage2 = []
    for d in range(1, 16):
        zz = (z + d) % 16
        stage2.append(remote(send2.at[zz], recv2.at[z], send2_sem.at[d], recv2_sem.at[d], peer2(zz)))
        stage2[-1].start()
    recv2[z] = send2[z]
    loads[0].wait()
    loads[1].wait()
    loads[2].wait()
    for c in stage2:
        c.wait_recv()

    x = recv2[...].reshape(256, 128)
    a = jnp.dot(first[0], x, preferred_element_type=F32) + jnp.dot(first[1], x, preferred_element_type=F32)
    ac, as_ = a[:256], a[256:]
    tc, ts = twiddle[0], twiddle[1]
    bre, bim = ac * tc - as_ * ts, ac * ts + as_ * tc
    b = jnp.concatenate([v[64 * k : 64 * k + 64] for k in range(4) for v in (bre, bim)], axis=1)
    bhigh = b.astype(BF16)
    blow = (b - bhigh.astype(F32)).astype(BF16)
    spectrum = (
        jnp.dot(bhigh, second[0], preferred_element_type=F32)
        + jnp.dot(blow, second[0], preferred_element_type=F32)
        + jnp.dot(bhigh, second[1], preferred_element_type=F32)
    )
    re, im = spectrum[:, :128].reshape(8, 8, 128), spectrum[:, 128:].reshape(8, 8, 128)
    energy = jnp.sum(jnp.sum(re * re + im * im, axis=0), axis=1, keepdims=True)
    scale = lax.rsqrt(energy + 1e-06)
    for k in range(8):
        units[8, :, 128 * k : 128 * k + 128] = jnp.concatenate([re[k] * scale, im[k] * scale], axis=0).astype(BF16)

    mine = units.at[8]

    @pl.when(jnp.logical_or(q == 0, q == 3))
    def _():
        low = q == 0
        lane0 = jnp.where(low, 0, 2)
        own_to = jnp.where(low, me + 8, me + 56) % 128
        opp_to = jnp.where(low, me + 72, me + 120) % 128
        for k in range(2):
            remote(mine, units.at[OWN], sende_sem.at[k], recvu_sem.at[OWN], own_to, lane0 + k).start()
        for k in range(2):
            remote(mine, units.at[OPP], sende_sem.at[2 + k], recvu_sem.at[OPP], opp_to, lane0 + k).start()

    window = {}
    for m in (7, 9, 6, 10, 5, 11, 4, 12, 3, 13, 2, 14, 1, 15, 0):
        window[m] = remote(mine, units.at[m], sendu_sem.at[m], recvu_sem.at[m], (me + 136 - m) % 128)
        window[m].start()

    def arrived(slot):
        remote(mine, units.at[slot], sende_sem.at[0], recvu_sem.at[slot], own_from, edge).wait_recv()

    arrived(OWN)
    own = units[OWN].astype(F32)
    for i in range(8):
        for c in range(2):
            wide[c, i] = jnp.broadcast_to(own[8 * c + i : 8 * c + i + 1], (8, 1024))

    def products(slot):
        v = units[slot].astype(F32)
        v0, v1 = v[:8], v[8:]
        for i in range(0, 8, 2):
            real = [wide[0, i + j] * v0 + wide[1, i + j] * v1 for j in range(2)]
            imag = [wide[1, i + j] * v0 - wide[0, i + j] * v1 for j in range(2)]
            lhs[slot, 8 * i : 8 * i + 16, :1024] = jnp.concatenate(real, axis=0).astype(BF16)
            lhs[slot, 8 * i : 8 * i + 16, 1024:] = jnp.concatenate(imag, axis=0).astype(BF16)

    loads[3].wait()
    for chunk in (2, 1, 3, 0):
        for m in range(4 * chunk, 4 * chunk + 4):
            if m != 8:
                window[m].wait_recv()

        @pl.loop(4 * chunk, 4 * chunk + 4)
        def _(m):
            products(m)

        cross[256 * chunk : 256 * chunk + 256] = jnp.dot(
            lhs[4 * chunk : 4 * chunk + 4].reshape(256, 2048), lag[...], preferred_element_type=F32
        )
    arrived(OPP)
    products(OPP)
    far = jnp.dot(lhs[OPP], lag[...], preferred_element_type=F32)
    out = far[:, 192:]
    for k in range(3):
        out = jnp.where(q == k, far[:, 64 * k : 64 * k + 64], out)
    opposite[...] = out

    for c in stage1 + stage2 + list(window.values()):
        c.wait_send()

    @pl.when(jnp.logical_or(q == 0, q == 3))
    def _():
        for k in range(4):
            remote(mine, units.at[OWN], sende_sem.at[k], recvu_sem.at[OWN], own_from, edge).wait_send()


def body(series, assign):
    first, twiddle, second, lag = tables()
    vmem = pl.BlockSpec(memory_space=pltpu.VMEM)
    hbm = pl.BlockSpec(memory_space=pl.ANY)
    dma = pltpu.SemaphoreType.DMA
    cross, opposite = pl.pallas_call(
        kernel,
        out_shape=[jax.ShapeDtypeStruct((1024, 256), F32), jax.ShapeDtypeStruct((64, 64), F32)],
        in_specs=[vmem] * 2 + [hbm] * 4,
        out_specs=[vmem] * 2,
        scratch_shapes=[
            pltpu.VMEM(first.shape, BF16),
            pltpu.VMEM(twiddle.shape, F32),
            pltpu.VMEM(second.shape, BF16),
            pltpu.VMEM(lag.shape, BF16),
            pltpu.VMEM((8, 32, 128), BF16),
            pltpu.VMEM((8, 32, 128), BF16),
            pltpu.VMEM((16, 16, 128), BF16),
            pltpu.VMEM((16, 16, 128), BF16),
            pltpu.VMEM((18, 16, 1024), BF16),
            pltpu.VMEM((2, 8, 8, 1024), F32),
            pltpu.VMEM((18, 64, 2048), BF16),
            dma((4,)), dma((8,)), dma((8,)), dma((16,)), dma((16,)), dma((16,)), dma((18,)), dma((4,)),
        ],
        compiler_params=pltpu.CompilerParams(
            collective_id=0, has_side_effects=True, vmem_limit_bytes=40 * 1024 * 1024
        ),
    )(series.T, assign.reshape(8, 128), first, twiddle, second, lag)
    return cross.reshape(1, 1, 16, 8, 8, 256), opposite.reshape(1, 8, 8, 64)


def solution(mesh):
    in_specs = (P(None, "blk"), P())
    out_specs = (P("blk", "pair", None, None, None, None), P("blk", None, None, "pair"))
    return jax.shard_map(body, mesh=mesh, in_specs=in_specs, out_specs=out_specs, check_vma=False)
```

time: 294 us -> 50.5 us (0.17)
  the two profiles are of different devices: /device:TPU:4 before, /device:TPU:2 now
where the time goes in v1:
time: 50.5 us; the launch traced here: 50.2 us
  Pallas kernels  42 us (83%)
  local copies, waits for them, and re-layouts  7.55 us (15%)
  between operations  0.65 us (1%)
    pallas_call x1, Pallas kernels, body(): pl.pallas_call(kernel, out_shape=[jax.ShapeDtypeStruct((1024, 256), F32),...  42 us
    unnamed x14, local copies, waits for them, and re-layouts  7.55 us

profile of v1, /device:TPU:2, one launch (start us, length us, event | category | flops | bytes accessed | tf_op | source)
XLA Modules:
  0.0 50.2 jit_solution(2536561816270706918)
XLA Ops:
  0.6 0.0 copy-start
  0.6 1.2 %copy-done = bf16[2048,256]{1,0:T(8,128)(2,1)S(1)} copy-done((bf16[2048,256]{1,0:T(8,128)(2,1)S(1)}, bf16[2048,256]{1,0:T(8,128)(2,1)}, u32[]{:S(2)}) %copy-start) | copy-done | bytes 1048600
  1.9 0.0 copy-start.1
  1.9 1.2 %copy-done.1 = bf16[2,1024,256]{2,1,0:T(8,128)(2,1)S(1)} copy-done((bf16[2,1024,256]{2,1,0:T(8,128)(2,1)S(1)}, bf16[2,1024,256]{2,1,0:T(8,128)(2,1)}, u32[]{:S(2)}) %copy-start.1) | copy-done | bytes 1048600
  3.1 0.0 copy-start.2
  3.1 1.0 %copy-done.2 = bf16[2,512,256]{2,1,0:T(8,128)(2,1)S(1)} copy-done((bf16[2,512,256]{2,1,0:T(8,128)(2,1)S(1)}, bf16[2,512,256]{2,1,0:T(8,128)(2,1)}, u32[]{:S(2)}) %copy-start.2) | copy-done | bytes 524312
  4.1 0.0 copy-start.3
  4.1 0.9 %copy-done.3 = f32[2,256,128]{2,1,0:T(8,128)S(1)} copy-done((f32[2,256,128]{2,1,0:T(8,128)S(1)}, f32[2,256,128]{2,1,0:T(8,128)}, u32[]{:S(2)}) %copy-start.3) | copy-done | bytes 262168
  5.1 0.0 copy-start.4
  5.1 0.8 %copy-done.4 = bf16[1024,32]{0,1:T(8,128)(2,1)S(1)} copy-done((bf16[1024,32]{0,1:T(8,128)(2,1)S(1)}, bf16[1024,32]{0,1:T(8,128)(2,1)}, u32[]{:S(2)}) %copy-start.4) | copy-done | bytes 65560
  5.9 0.0 copy-start.5
  5.9 0.7 %copy-done.5 = s32[1024]{0:T(1024)S(1)} copy-done((s32[1024]{0:T(1024)S(1)}, s32[1024]{0:T(1024)}, u32[]{:S(2)}) %copy-start.5) | copy-done | bytes 4120
  6.6 42.0 %shard_map.77 = (f32[1024,256]{1,0:T(8,128)S(1)}, f32[64,64]{1,0:T(8,128)S(1)}) custom-call(bf16[32,1024]{1,0:T(8,128)(2,1)S(1)} %bitcast.5, s32[8,128]{1,0:T(8,128)S(1)} %bitcast.7, bf16[2,512,256]{2,1,0:T(8,128)(2,1)S(1)} %copy-done.2, f32[2,256,128]{2,1,0:T(8,128)S(1)} %copy-done.3, bf16[2,1024,256]{2,1,0:T(8,128)(2,1)S(1)} %copy-done.1, ...), custom_call_target="tpu_custom_call" | custom-call | tf_op jit(solution)/shard_map/pallas_call | solution.py:249
  48.6 1.0 %copy.10 = f32[1,1,16,8,8,256]{5,4,3,2,1,0:T(8,128)} copy(f32[1,1,16,8,8,256]{5,4,3,2,1,0:T(8,128)S(1)} %bitcast.4) | data formatting | bytes 2097152
  49.6 0.6 %copy.11 = f32[1,8,8,64]{3,2,1,0:T(8,128)} copy(f32[1,8,8,64]{3,2,1,0:T(8,128)S(1)} %bitcast.6) | data formatting | bytes 32768
Async XLA Ops:
  0.6 1.2 %copy-start = (bf16[2048,256]{1,0:T(8,128)(2,1)S(1)}, bf16[2048,256]{1,0:T(8,128)(2,1)}, u32[]{:S(2)}) copy-start(bf16[2048,256]{1,0:T(8,128)(2,1)} %constant.11.clone.lag_hbm) | copy-start | bytes 3145732
  1.9 1.2 %copy-start.1 = (bf16[2,1024,256]{2,1,0:T(8,128)(2,1)S(1)}, bf16[2,1024,256]{2,1,0:T(8,128)(2,1)}, u32[]{:S(2)}) copy-start(bf16[2,1024,256]{2,1,0:T(8,128)(2,1)} %constant.10.clone.second_hbm) | copy-start | bytes 3145732
  3.1 1.0 %copy-start.2 = (bf16[2,512,256]{2,1,0:T(8,128)(2,1)S(1)}, bf16[2,512,256]{2,1,0:T(8,128)(2,1)}, u32[]{:S(2)}) copy-start(bf16[2,512,256]{2,1,0:T(8,128)(2,1)} %constant.8.clone.first_hbm) | copy-start | bytes 1572868
  4.1 0.9 %copy-start.3 = (f32[2,256,128]{2,1,0:T(8,128)S(1)}, f32[2,256,128]{2,1,0:T(8,128)}, u32[]{:S(2)}) copy-start(f32[2,256,128]{2,1,0:T(8,128)} %constant.9.clone.twiddle_hbm) | copy-start | bytes 786436
  5.1 0.8 %copy-start.4 = (bf16[1024,32]{0,1:T(8,128)(2,1)S(1)}, bf16[1024,32]{0,1:T(8,128)(2,1)}, u32[]{:S(2)}) copy-start(bf16[1024,32]{0,1:T(8,128)(2,1)} %param.6) | copy-start | bytes 196612
  5.9 0.7 %copy-start.5 = (s32[1024]{0:T(1024)S(1)}, s32[1024]{0:T(1024)}, u32[]{:S(2)}) copy-start(s32[1024]{0:T(1024)} %param.7) | copy-start | bytes 12292

commit v2 on v1

v2 whole, which is shorter than its diff:
```python
import math

import jax
import jax.numpy as jnp
import ml_dtypes
import numpy as np
from jax import lax
from jax.experimental import pallas as pl
from jax.experimental.pallas import tpu as pltpu
from jax.sharding import PartitionSpec as P

F32 = jnp.float32
BF16 = jnp.bfloat16
MESH = pl.DeviceIdType.MESH
N = 4096
PASS, OWN, OPP = 16, 17, 18


def two_parts(x):
    high = x.astype(ml_dtypes.bfloat16)
    low = (x - high.astype(np.float64)).astype(ml_dtypes.bfloat16)
    return np.stack([high, low])


def tables():
    k1 = np.arange(32)
    z, h = np.arange(16), np.arange(2)
    n1 = 16 * h[None, :] + z[:, None]
    angle = 2 * np.pi * ((k1[:, None, None] + 1) * n1[None] % 32) / 32
    first = np.stack([np.cos(angle), np.sin(angle)]) / math.sqrt(N)
    first = np.einsum("ckzh,pr->ckpzhr", first, np.eye(8)).reshape(512, 256)
    n2 = np.arange(128)
    angle = 2 * np.pi * ((k1[:, None] + 1) * n2[None] % N) / N
    twiddle = np.stack([np.cos(angle), np.sin(angle)])
    twiddle = np.repeat(twiddle, 8, axis=1).astype(np.float32)
    k2 = np.arange(32)
    angle = 2 * np.pi * (n2[:, None] * k2[None] % 128) / 128
    co, si = np.cos(angle), np.sin(angle)
    second = np.array([[co, si], [-si, co]])
    second = np.einsum("rcnk,ab->arncbk", second, np.eye(4)).reshape(1024, 256)
    k1b, k1a = np.arange(8), np.arange(4)
    k = 1 + 8 * k1a[None, :, None] + k1b[:, None, None] + 32 * k2[None, None, :]
    shift = np.arange(256) - 128
    angle = 2 * np.pi * (k.reshape(1024)[:, None] * shift[None] % N) / N
    lag = np.concatenate([np.cos(angle), -np.sin(angle)]).astype(ml_dtypes.bfloat16)
    return two_parts(first), twiddle, two_parts(second), lag


def kernel(
    series_hbm, assign_hbm, first_hbm, twiddle_hbm, second_hbm, lag_hbm,
    cross, opposite,
    series, assign, first, twiddle, second, lag, send1, recv1, send2, recv2, units, wide, lhs,
    load_sem, send1_sem, recv1_sem, send2_sem, recv2_sem, sendu_sem, recvu_sem, near_sem, far_sem,
):
    me, q = lax.axis_index("blk"), lax.axis_index("pair")
    half, z, y = me // 64, me // 4 % 16, me % 4
    spot = half * 4 + y

    def device(blk, pair=None):
        return {"blk": blk, "pair": q if pair is None else pair}

    def peer1(s):
        return s // 4 * 64 + z * 4 + s % 4

    def peer2(zz):
        return half * 64 + zz * 4 + y

    loads = [
        pltpu.make_async_copy(src, dst, load_sem.at[i])
        for i, (src, dst) in enumerate(
            [(first_hbm, first), (twiddle_hbm, twiddle), (second_hbm, second), (lag_hbm, lag),
             (assign_hbm, assign), (series_hbm, series)]
        )
    ]
    for c in loads[::-1]:
        c.start()

    barrier = pltpu.get_barrier_semaphore()
    core = q % 2
    other = q + 1 - 2 * core

    def greet(blk, pair):
        pl.semaphore_signal(barrier, 1, device_id=device(blk, pair), device_id_type=MESH)

    greet(me, other)
    for d in range(1, 8):
        greet(peer1((spot + d) % 8), q - core + 1)
    for d in range(1, 16):
        greet(peer2((z + d) % 16), q - core)
    for d in (4, 8, 120, 124):
        greet((me + d) % 128, q - core)

    @pl.when(q >= 2)
    def _():
        greet(me, 0)
        greet((me + 64) % 128, 0)

    @pl.when(core == 1)
    def _():
        pl.semaphore_wait(barrier, 1 + 2 * 7)
        pl.semaphore_signal(near_sem, 1, device_id=device(me, other), device_id_type=MESH)

    loads[4].wait()
    ids = assign[...]
    turned = pltpu.roll(ids, 64, 1)
    rows = [turned] + [pltpu.roll(turned, 8 - k, 0) for k in range(1, 5)]

    def pick(first_row):
        out = rows[first_row + 3]
        for k in (2, 1, 0):
            out = jnp.where(q == k, rows[first_row + k], out)
        return out

    lane = lax.broadcasted_iota(jnp.int32, (8, 128), 1)
    row = lax.broadcasted_iota(jnp.int32, (8, 128), 0)
    moved = jnp.where(lane < 64, pick(0), pick(1))
    wanted = {}
    for yy in range(4):
        index = lane // 8 % 4 * 32 + yy * 8 + lane % 8
        got = jnp.take_along_axis(moved, index, axis=1)
        got = jnp.where(lane // 32 == row % 4, got, 0)
        for hh in range(2):
            wanted[hh * 4 + yy] = jnp.sum(got[hh * 4 : hh * 4 + 4], axis=0, keepdims=True)

    loads[5].wait()
    samples = series[...].astype(F32)
    for s in range(8):
        ids = jnp.broadcast_to(wanted[s], (32, 128))
        source, index = ids // 128, ids % 128
        part = jnp.zeros((32, 128), F32)
        for k in range(8):
            got = jnp.take_along_axis(samples[:, 128 * k : 128 * k + 128], index, axis=1)
            part = jnp.where(source == k, got, part)
        send1[s] = part.astype(BF16)

    @pl.when(core == 0)
    def _():
        pl.semaphore_wait(near_sem, 1)

    def remote(src, dst, ssem, rsem, blk, pair=None):
        return pltpu.make_async_remote_copy(
            src_ref=src, dst_ref=dst, send_sem=ssem, recv_sem=rsem,
            device_id=device(blk, pair), device_id_type=MESH,
        )

    stage1 = []
    for d in (6, 5, 7, 2, 4, 1, 3):
        s = (spot + d) % 8
        stage1.append(remote(send1.at[s], recv1.at[spot], send1_sem.at[d], recv1_sem.at[d], peer1(s)))
        stage1[-1].start()
    recv1[spot] = send1[spot]

    @pl.when(core == 0)
    def _():
        pl.semaphore_wait(barrier, 1 + 2 * (15 + 4) + jnp.where(q == 0, 4, 0))
        pl.semaphore_signal(far_sem, 1, device_id=device(me, other), device_id_type=MESH)

    for c in stage1:
        c.wait_recv()
    sides = []
    for hh in range(2):
        side = recv1[hh * 4 : hh * 4 + 4].reshape(128, 128).astype(F32)
        sides.append(jnp.transpose(side).reshape(16, 8, 128))
    send2[...] = jnp.concatenate(sides, axis=1).astype(BF16)

    @pl.when(core == 1)
    def _():
        pl.semaphore_wait(far_sem, 1)

    stage2 = []
    for d in (8, 7, 9, 6, 10, 5, 11, 4, 12, 3, 13, 2, 14, 1, 15):
        zz = (z + d) % 16
        stage2.append(remote(send2.at[zz], recv2.at[z], send2_sem.at[d], recv2_sem.at[d], peer2(zz)))
        stage2[-1].start()
    recv2[z] = send2[z]
    loads[0].wait()
    loads[1].wait()
    loads[2].wait()
    for c in stage2:
        c.wait_recv()

    x = recv2[...].reshape(256, 128)
    a = jnp.dot(first[0], x, preferred_element_type=F32) + jnp.dot(first[1], x, preferred_element_type=F32)
    ac, as_ = a[:256], a[256:]
    tc, ts = twiddle[0], twiddle[1]
    bre, bim = ac * tc - as_ * ts, ac * ts + as_ * tc
    b = jnp.concatenate([v[64 * k : 64 * k + 64] for k in range(4) for v in (bre, bim)], axis=1)
    bhigh = b.astype(BF16)
    blow = (b - bhigh.astype(F32)).astype(BF16)
    spectrum = (
        jnp.dot(bhigh, second[0], preferred_element_type=F32)
        + jnp.dot(blow, second[0], preferred_element_type=F32)
        + jnp.dot(bhigh, second[1], preferred_element_type=F32)
    )
    re, im = spectrum[:, :128].reshape(8, 8, 128), spectrum[:, 128:].reshape(8, 8, 128)
    energy = jnp.sum(jnp.sum(re * re + im * im, axis=0), axis=1, keepdims=True)
    scale = lax.rsqrt(energy + 1e-06)
    for k in range(8):
        units[8 + y, :, 128 * k : 128 * k + 128] = jnp.concatenate([re[k] * scale, im[k] * scale], axis=0).astype(BF16)

    mine = units.at[8 + y]
    sent = []

    def send(src, slot, blk, pair=None):
        sem = sendu_sem.at[len(sent)]
        sent.append(remote(src, units.at[slot], sem, recvu_sem.at[slot], blk, pair))
        return sent[-1]

    def arrived(slot):
        remote(mine, units.at[slot], sendu_sem.at[0], recvu_sem.at[slot], (me + 4) % 128).wait_recv()

    up2, down2 = (me + 8) % 128, (me + 120) % 128
    up1, down1 = (me + 4) % 128, (me + 124) % 128
    column = {k: (y + k) % 4 for k in (1, 2, 3)}
    slab = me // 4 * 4
    to_up2 = send(mine, y, up2)
    to_down2 = send(mine, PASS, down2)
    to_up2.start()
    send(mine, 8 + y, slab + column[2]).start()

    @pl.when(y < 3)
    def _():
        to_down2.start()

    send(mine, 8 + y, slab + column[1]).start()
    send(mine, 8 + y, slab + column[3]).start()
    send(mine, 4 + y, up1).start()
    send(mine, 12 + y, down1).start()
    for k in (1, 3):
        arrived(8 + column[k])
        send(units.at[8 + column[k]], 4 + column[k], up1).start()
        send(units.at[8 + column[k]], 12 + column[k], down1).start()
    arrived(y)
    extras = [send(units.at[y], OWN, me, lane) for lane in (2, 3, 1)]
    extras += [send(units.at[y], OPP, (me + 64) % 128, lane) for lane in (2, 3, 0, 1)]

    @pl.when(q == 0)
    def _():
        for c in extras:
            c.start()

    @pl.when(y < 3)
    def _():
        arrived(PASS)

    for k in (2, 1, 3):
        send(units.at[jnp.where(column[k] < y, y, PASS)], y, slab + column[k]).start()
    arrived(8 + column[2])
    send(units.at[8 + column[2]], 4 + column[2], up1).start()
    send(units.at[8 + column[2]], 12 + column[2], down1).start()

    @pl.when(q > 0)
    def _():
        arrived(OWN)

    own = units[jnp.where(q == 0, y, OWN)].astype(F32)
    for i in range(8):
        for c in range(2):
            wide[c, i] = jnp.broadcast_to(own[8 * c + i : 8 * c + i + 1], (8, 1024))

    def products(slot):
        v = units[slot].astype(F32)
        v0, v1 = v[:8], v[8:]
        for i in range(0, 8, 2):
            real = [wide[0, i + j] * v0 + wide[1, i + j] * v1 for j in range(2)]
            imag = [wide[1, i + j] * v0 - wide[0, i + j] * v1 for j in range(2)]
            lhs[slot, 8 * i : 8 * i + 16, :1024] = jnp.concatenate(real, axis=0).astype(BF16)
            lhs[slot, 8 * i : 8 * i + 16, 1024:] = jnp.concatenate(imag, axis=0).astype(BF16)

    loads[3].wait()

    def chunk(first_slot):
        for slot in range(first_slot, first_slot + 4):
            products(slot)
        rows = lhs[first_slot : first_slot + 4].reshape(256, 2048)
        return jnp.dot(rows, lag[...], preferred_element_type=F32).reshape(4, 64, 256)

    cross[pl.ds(8 - y, 4)] = chunk(8)
    for first_slot in (4, 12):
        for k in range(4):
            arrived(first_slot + k)
        cross[pl.ds(first_slot - y, 4)] = chunk(first_slot)
    arrived(OPP)
    products(OPP)
    far = jnp.dot(lhs[OPP], lag[...], preferred_element_type=F32)
    out = far[:, 192:]
    for k in range(3):
        out = jnp.where(q == k, far[:, 64 * k : 64 * k + 64], out)
    opposite[...] = out
    for k in (1, 2, 3):
        arrived(column[k])
    ends = chunk(0)
    for k in range(4):
        cross[(k - y + 16) % 16] = ends[k]

    for c in stage1 + stage2:
        c.wait_send()
    special = [id(c) for c in [to_down2] + extras]
    for c in sent:
        if id(c) not in special:
            c.wait_send()

    @pl.when(y < 3)
    def _():
        to_down2.wait_send()

    @pl.when(q == 0)
    def _():
        for c in extras:
            c.wait_send()


def finish(cross, opposite, cross_out, opposite_out, sem):
    copies = [
        pltpu.make_async_copy(cross, cross_out, sem.at[0]),
        pltpu.make_async_copy(opposite, opposite_out, sem.at[1]),
    ]
    for c in copies:
        c.start()
    for c in copies:
        c.wait()


def body(series, assign):
    first, twiddle, second, lag = tables()
    vmem = pl.BlockSpec(memory_space=pltpu.VMEM)
    hbm = pl.BlockSpec(memory_space=pltpu.HBM)
    dma = pltpu.SemaphoreType.DMA
    cross, opposite = pl.pallas_call(
        kernel,
        out_shape=[pltpu.VMEM((16, 64, 256), F32), pltpu.VMEM((64, 64), F32)],
        in_specs=[hbm] * 6,
        out_specs=[vmem] * 2,
        scratch_shapes=[
            pltpu.VMEM((32, 1024), BF16),
            pltpu.VMEM((8, 128), jnp.int32),
            pltpu.VMEM(first.shape, BF16),
            pltpu.VMEM(twiddle.shape, F32),
            pltpu.VMEM(second.shape, BF16),
            pltpu.VMEM(lag.shape, BF16),
            pltpu.VMEM((8, 32, 128), BF16),
            pltpu.VMEM((8, 32, 128), BF16),
            pltpu.VMEM((16, 16, 128), BF16),
            pltpu.VMEM((16, 16, 128), BF16),
            pltpu.VMEM((19, 16, 1024), BF16),
            pltpu.VMEM((2, 8, 8, 1024), F32),
            pltpu.VMEM((19, 64, 2048), BF16),
            dma((6,)), dma((8,)), dma((8,)), dma((16,)), dma((16,)), dma((23,)), dma((19,)),
            pltpu.SemaphoreType.REGULAR, pltpu.SemaphoreType.REGULAR,
        ],
        compiler_params=pltpu.CompilerParams(
            collective_id=0, has_side_effects=True, vmem_limit_bytes=60 * 1024 * 1024
        ),
    )(series.T, assign.reshape(8, 128), first, twiddle, second, lag)
    cross, opposite = pl.pallas_call(
        finish,
        out_shape=[jax.ShapeDtypeStruct((16, 64, 256), F32), jax.ShapeDtypeStruct((64, 64), F32)],
        in_specs=[vmem] * 2,
        out_specs=[pl.BlockSpec(memory_space=pltpu.HBM)] * 2,
        scratch_shapes=[dma((2,))],
        compiler_params=pltpu.CompilerParams(vmem_limit_bytes=2 * 1024 * 1024),
    )(cross, opposite)
    return cross.reshape(1, 1, 16, 8, 8, 256), opposite.reshape(1, 8, 8, 64)


def solution(mesh):
    in_specs = (P(None, "blk"), P())
    out_specs = (P("blk", "pair", None, None, None, None), P("blk", None, None, "pair"))
    return jax.shard_map(body, mesh=mesh, in_specs=in_specs, out_specs=out_specs, check_vma=False)
```

time: 50.5 us -> 39.8 us (0.79)
  the two profiles are of different devices: /device:TPU:2 before, /device:TPU:7 now
where the time goes in v2:
time: 39.8 us; the launch traced here: 39.6 us
  Pallas kernels  39 us (98%)
  between operations  0.64 us (2%)
    pallas_call x1, Pallas kernels, body(): pl.pallas_call(kernel, out_shape=[pltpu.VMEM((16, 64, 256), F32), pltpu.V...  38 us
    pallas_call x1, Pallas kernels, body(): pl.pallas_call(finish, out_shape=[jax.ShapeDtypeStruct((16, 64, 256), F32...  0.99 us

profile of v2, /device:TPU:7, one launch (start us, length us, event | category | flops | bytes accessed | tf_op | source)
XLA Modules:
  0.0 39.6 jit_solution(15754987359531166571)
XLA Ops:
  0.6 38.0 %shard_map.77 = (f32[16,64,256]{2,1,0:T(8,128)S(1)}, f32[64,64]{1,0:T(8,128)S(1)}) custom-call(bf16[32,1024]{1,0:T(8,128)(2,1)} %bitcast.4, s32[8,128]{1,0:T(8,128)} %bitcast.5, bf16[2,512,256]{2,1,0:T(8,128)(2,1)} %constant.8.clone.first_hbm, f32[2,256,128]{2,1,0:T(8,128)} %constant.9.clone.twiddle_hbm, bf16[2,1024,256]{2,1,0:T(8,128)(2,1)} %constant.10.clone.second_hbm, ...), custom_call_target="tpu_custom_call" | custom-call | tf_op jit(solution)/shard_map/pallas_call | solution.py:329
  38.6 1.0 %shard_map.78 = (f32[16,64,256]{2,1,0:T(8,128)}, f32[64,64]{1,0:T(8,128)}) custom-call(f32[16,64,256]{2,1,0:T(8,128)S(1)} %get-tuple-element.6.cross, f32[64,64]{1,0:T(8,128)S(1)} %get-tuple-element.7.opposite), custom_call_target="tpu_custom_call" | custom-call | tf_op jit(solution)/shard_map/pallas_call | solution.py:355

commit v3 on v2

--- a/solution.py
+++ b/solution.py
@@ -82,18 +82,23 @@
     def greet(blk, pair):
         pl.semaphore_signal(barrier, 1, device_id=device(blk, pair), device_id_type=MESH)
 
+    slab = me // 4 * 4
+    up1, down1, up2, down2 = (slab + 4) % 128, (slab + 124) % 128, (slab + 8) % 128, (slab + 120) % 128
+    column = {k: (y + k) % 4 for k in (1, 2, 3)}
     greet(me, other)
+    for d in (8, 7, 9, 6, 10, 5, 11, 4, 12, 3, 13, 2, 14, 1, 15):
+        greet(peer2((z + d) % 16), q - core)
     for d in range(1, 8):
         greet(peer1((spot + d) % 8), q - core + 1)
-    for d in range(1, 16):
-        greet(peer2((z + d) % 16), q - core)
-    for d in (4, 8, 120, 124):
-        greet((me + d) % 128, q - core)
+    for blk in (up1, down1, up2, down2):
+        greet(blk + y, q - core)
+    for blk in (up1, down1):
+        for k in (1, 3):
+            greet(blk + column[k], q - core)
 
     @pl.when(q >= 2)
     def _():
-        greet(me, 0)
-        greet((me + 64) % 128, 0)
+        greet((me + 72) % 128, 2)
 
     @pl.when(core == 1)
     def _():
@@ -152,7 +157,7 @@
 
     @pl.when(core == 0)
     def _():
-        pl.semaphore_wait(barrier, 1 + 2 * (15 + 4) + jnp.where(q == 0, 4, 0))
+        pl.semaphore_wait(barrier, 1 + 2 * (15 + 4 + 4) + jnp.where(q == 2, 2, 0))
         pl.semaphore_signal(far_sem, 1, device_id=device(me, other), device_id_type=MESH)
 
     for c in stage1:
@@ -209,35 +214,38 @@
     def arrived(slot):
         remote(mine, units.at[slot], sendu_sem.at[0], recvu_sem.at[slot], (me + 4) % 128).wait_recv()
 
-    up2, down2 = (me + 8) % 128, (me + 120) % 128
-    up1, down1 = (me + 4) % 128, (me + 124) % 128
-    column = {k: (y + k) % 4 for k in (1, 2, 3)}
-    slab = me // 4 * 4
-    to_up2 = send(mine, y, up2)
-    to_down2 = send(mine, PASS, down2)
+    to_up2 = send(mine, y, up2 + y)
+    to_own = [send(mine, OWN, up2 + y, 1)] + [send(mine, OWN, (me + 56) % 128, lane) for lane in (2, 3)]
+    to_down2 = send(mine, PASS, down2 + y)
     to_up2.start()
+
+    @pl.when(q == 0)
+    def _():
+        to_own[0].start()
+
+    @pl.when(q == 3)
+    def _():
+        to_own[1].start()
+        to_own[2].start()
+
     send(mine, 8 + y, slab + column[2]).start()
 
     @pl.when(y < 3)
     def _():
         to_down2.start()
 
-    send(mine, 8 + y, slab + column[1]).start()
-    send(mine, 8 + y, slab + column[3]).start()
-    send(mine, 4 + y, up1).start()
-    send(mine, 12 + y, down1).start()
     for k in (1, 3):
-        arrived(8 + column[k])
-        send(units.at[8 + column[k]], 4 + column[k], up1).start()
-        send(units.at[8 + column[k]], 12 + column[k], down1).start()
+        send(mine, 8 + y, slab + column[k]).start()
+    send(mine, 4 + y, up1 + y).start()
+    send(mine, 12 + y, down1 + y).start()
+    for k in (1, 3):
+        send(mine, 4 + y, up1 + column[k]).start()
+        send(mine, 12 + y, down1 + column[k]).start()
+
+    arrived(8 + column[2])
+    send(units.at[8 + column[2]], 4 + column[2], up1 + y).start()
+    send(units.at[8 + column[2]], 12 + column[2], down1 + y).start()
     arrived(y)
-    extras = [send(units.at[y], OWN, me, lane) for lane in (2, 3, 1)]
-    extras += [send(units.at[y], OPP, (me + 64) % 128, lane) for lane in (2, 3, 0, 1)]
-
-    @pl.when(q == 0)
-    def _():
-        for c in extras:
-            c.start()
 
     @pl.when(y < 3)
     def _():
@@ -245,57 +253,61 @@
 
     for k in (2, 1, 3):
         send(units.at[jnp.where(column[k] < y, y, PASS)], y, slab + column[k]).start()
-    arrived(8 + column[2])
-    send(units.at[8 + column[2]], 4 + column[2], up1).start()
-    send(units.at[8 + column[2]], 12 + column[2], down1).start()
 
     @pl.when(q > 0)
     def _():
         arrived(OWN)
 
-    own = units[jnp.where(q == 0, y, OWN)].astype(F32)
+    own_slot = jnp.where(q == 0, y, OWN)
+    send(units.at[own_slot], OPP, (me + 64) % 128).start()
+    own = units[own_slot].astype(F32)
     for i in range(8):
         for c in range(2):
             wide[c, i] = jnp.broadcast_to(own[8 * c + i : 8 * c + i + 1], (8, 1024))
 
-    def products(slot):
+    def products(slot, spot):
         v = units[slot].astype(F32)
         v0, v1 = v[:8], v[8:]
         for i in range(0, 8, 2):
             real = [wide[0, i + j] * v0 + wide[1, i + j] * v1 for j in range(2)]
             imag = [wide[1, i + j] * v0 - wide[0, i + j] * v1 for j in range(2)]
-            lhs[slot, 8 * i : 8 * i + 16, :1024] = jnp.concatenate(real, axis=0).astype(BF16)
-            lhs[slot, 8 * i : 8 * i + 16, 1024:] = jnp.concatenate(imag, axis=0).astype(BF16)
+            lhs[spot, 8 * i : 8 * i + 16, :1024] = jnp.concatenate(real, axis=0).astype(BF16)
+            lhs[spot, 8 * i : 8 * i + 16, 1024:] = jnp.concatenate(imag, axis=0).astype(BF16)
+
+    def correlate(first_spot, slots):
+        for k, slot in enumerate(slots):
+            products(slot, first_spot + k)
+        rows = lhs[first_spot : first_spot + len(slots)].reshape(64 * len(slots), 2048)
+        out = jnp.dot(rows, lag[...], preferred_element_type=F32)
+        for k, slot in enumerate(slots):
+            if not isinstance(slot, int) or slot != OPP:
+                cross[(slot - y + 16) % 16] = out[64 * k : 64 * k + 64]
+        return out
 
     loads[3].wait()
-
-    def chunk(first_slot):
-        for slot in range(first_slot, first_slot + 4):
-            products(slot)
-        rows = lhs[first_slot : first_slot + 4].reshape(256, 2048)
-        return jnp.dot(rows, lag[...], preferred_element_type=F32).reshape(4, 64, 256)
-
-    cross[pl.ds(8 - y, 4)] = chunk(8)
-    for first_slot in (4, 12):
-        for k in range(4):
-            arrived(first_slot + k)
-        cross[pl.ds(first_slot - y, 4)] = chunk(first_slot)
-    arrived(OPP)
-    products(OPP)
-    far = jnp.dot(lhs[OPP], lag[...], preferred_element_type=F32)
+    arrived(8 + column[1])
+    arrived(8 + column[3])
+    correlate(0, [8, 9, 10, 11])
+    near = [first + c for first in (4, 12) for c in (y, column[1], column[3])]
+    for slot in near:
+        arrived(slot)
+    correlate(4, [y] + near)
+    late = [4 + column[2], 12 + column[2]]
+    for slot in late + [OPP]:
+        arrived(slot)
+    far = correlate(11, late + [OPP])[128:]
     out = far[:, 192:]
     for k in range(3):
         out = jnp.where(q == k, far[:, 64 * k : 64 * k + 64], out)
     opposite[...] = out
-    for k in (1, 2, 3):
-        arrived(column[k])
-    ends = chunk(0)
-    for k in range(4):
-        cross[(k - y + 16) % 16] = ends[k]
+    edges = [column[k] for k in (1, 2, 3)]
+    for slot in edges:
+        arrived(slot)
+    correlate(14, edges)
 
     for c in stage1 + stage2:
         c.wait_send()
-    special = [id(c) for c in [to_down2] + extras]
+    special = [id(c) for c in [to_down2] + to_own]
     for c in sent:
         if id(c) not in special:
             c.wait_send()
@@ -306,8 +318,12 @@
 
     @pl.when(q == 0)
     def _():
-        for c in extras:
-            c.wait_send()
+        to_own[0].wait_send()
+
+    @pl.when(q == 3)
+    def _():
+        to_own[1].wait_send()
+        to_own[2].wait_send()
 
 
 def finish(cross, opposite, cross_out, opposite_out, sem):
@@ -344,7 +360,7 @@
             pltpu.VMEM((16, 16, 128), BF16),
             pltpu.VMEM((19, 16, 1024), BF16),
             pltpu.VMEM((2, 8, 8, 1024), F32),
-            pltpu.VMEM((19, 64, 2048), BF16),
+            pltpu.VMEM((17, 64, 2048), BF16),
             dma((6,)), dma((8,)), dma((8,)), dma((16,)), dma((16,)), dma((23,)), dma((19,)),
             pltpu.SemaphoreType.REGULAR, pltpu.SemaphoreType.REGULAR,
         ],

time: 39.8 us -> 36.9 us (0.927)
  the two profiles are of different devices: /device:TPU:7 before, /device:TPU:4 now
where the time goes in v3:
time: 36.9 us; the launch traced here: 36.7 us
  Pallas kernels  36.1 us (98%)
  between operations  0.64 us (2%)
    pallas_call x1, Pallas kernels, body(): pl.pallas_call(kernel, out_shape=[pltpu.VMEM((16, 64, 256), F32), pltpu.V...  35.1 us
    pallas_call x1, Pallas kernels, body(): pl.pallas_call(finish, out_shape=[jax.ShapeDtypeStruct((16, 64, 256), F32...  0.99 us

profile of v3, /device:TPU:4, one launch (start us, length us, event | category | flops | bytes accessed | tf_op | source)
XLA Modules:
  0.0 36.7 jit_solution(10742405311594739675)
XLA Ops:
  0.6 35.1 %shard_map.77 = (f32[16,64,256]{2,1,0:T(8,128)S(1)}, f32[64,64]{1,0:T(8,128)S(1)}) custom-call(bf16[32,1024]{1,0:T(8,128)(2,1)} %bitcast.4, s32[8,128]{1,0:T(8,128)} %bitcast.5, bf16[2,512,256]{2,1,0:T(8,128)(2,1)} %constant.8.clone.first_hbm, f32[2,256,128]{2,1,0:T(8,128)} %constant.9.clone.twiddle_hbm, bf16[2,1024,256]{2,1,0:T(8,128)(2,1)} %constant.10.clone.second_hbm, ...), custom_call_target="tpu_custom_call" | custom-call | tf_op jit(solution)/shard_map/pallas_call | solution.py:345
  35.8 1.0 %shard_map.78 = (f32[16,64,256]{2,1,0:T(8,128)}, f32[64,64]{1,0:T(8,128)}) custom-call(f32[16,64,256]{2,1,0:T(8,128)S(1)} %get-tuple-element.6.cross, f32[64,64]{1,0:T(8,128)S(1)} %get-tuple-element.7.opposite), custom_call_target="tpu_custom_call" | custom-call | tf_op jit(solution)/shard_map/pallas_call | solution.py:371

commit v4 on v3

--- a/solution.py
+++ b/solution.py
@@ -72,7 +72,7 @@
              (assign_hbm, assign), (series_hbm, series)]
         )
     ]
-    for c in loads[::-1]:
+    for c in loads[4:]:
         c.start()
 
     barrier = pltpu.get_barrier_semaphore()
@@ -96,7 +96,7 @@
         for k in (1, 3):
             greet(blk + column[k], q - core)
 
-    @pl.when(q >= 2)
+    @pl.when(q == 3)
     def _():
         greet((me + 72) % 128, 2)
 
@@ -121,17 +121,17 @@
     moved = jnp.where(lane < 64, pick(0), pick(1))
     wanted = {}
     for yy in range(4):
-        index = lane // 8 % 4 * 32 + yy * 8 + lane % 8
+        index = ((lane >> 3) & 3) * 32 + yy * 8 + (lane & 7)
         got = jnp.take_along_axis(moved, index, axis=1)
-        got = jnp.where(lane // 32 == row % 4, got, 0)
+        got = jnp.where((lane >> 5) == (row & 3), got, 0)
         for hh in range(2):
             wanted[hh * 4 + yy] = jnp.sum(got[hh * 4 : hh * 4 + 4], axis=0, keepdims=True)
 
     loads[5].wait()
     samples = series[...].astype(F32)
     for s in range(8):
-        ids = jnp.broadcast_to(wanted[s], (32, 128))
-        source, index = ids // 128, ids % 128
+        source = jnp.broadcast_to(wanted[s] >> 7, (32, 128))
+        index = jnp.broadcast_to(wanted[s] & 127, (32, 128))
         part = jnp.zeros((32, 128), F32)
         for k in range(8):
             got = jnp.take_along_axis(samples[:, 128 * k : 128 * k + 128], index, axis=1)
@@ -153,11 +153,13 @@
         s = (spot + d) % 8
         stage1.append(remote(send1.at[s], recv1.at[spot], send1_sem.at[d], recv1_sem.at[d], peer1(s)))
         stage1[-1].start()
+    for c in loads[:4]:
+        c.start()
     recv1[spot] = send1[spot]
 
     @pl.when(core == 0)
     def _():
-        pl.semaphore_wait(barrier, 1 + 2 * (15 + 4 + 4) + jnp.where(q == 2, 2, 0))
+        pl.semaphore_wait(barrier, 1 + 2 * (15 + 4 + 4) + jnp.where(q == 2, 1, 0))
         pl.semaphore_signal(far_sem, 1, device_id=device(me, other), device_id_type=MESH)
 
     for c in stage1:
@@ -192,11 +194,8 @@
     b = jnp.concatenate([v[64 * k : 64 * k + 64] for k in range(4) for v in (bre, bim)], axis=1)
     bhigh = b.astype(BF16)
     blow = (b - bhigh.astype(F32)).astype(BF16)
-    spectrum = (
-        jnp.dot(bhigh, second[0], preferred_element_type=F32)
-        + jnp.dot(blow, second[0], preferred_element_type=F32)
-        + jnp.dot(bhigh, second[1], preferred_element_type=F32)
-    )
+    both = jnp.dot(jnp.concatenate([bhigh, blow], axis=0), second[0], preferred_element_type=F32)
+    spectrum = both[:64] + both[64:] + jnp.dot(bhigh, second[1], preferred_element_type=F32)
     re, im = spectrum[:, :128].reshape(8, 8, 128), spectrum[:, 128:].reshape(8, 8, 128)
     energy = jnp.sum(jnp.sum(re * re + im * im, axis=0), axis=1, keepdims=True)
     scale = lax.rsqrt(energy + 1e-06)
@@ -215,8 +214,9 @@
         remote(mine, units.at[slot], sendu_sem.at[0], recvu_sem.at[slot], (me + 4) % 128).wait_recv()
 
     to_up2 = send(mine, y, up2 + y)
-    to_own = [send(mine, OWN, up2 + y, 1)] + [send(mine, OWN, (me + 56) % 128, lane) for lane in (2, 3)]
+    to_own = [send(mine, OWN, up2 + y, 1), send(mine, OWN, (me + 56) % 128, 3), send(units.at[OWN], OWN, me, 2)]
     to_down2 = send(mine, PASS, down2 + y)
+    send(mine, 8 + y, slab + column[2]).start()
     to_up2.start()
 
     @pl.when(q == 0)
@@ -226,9 +226,7 @@
     @pl.when(q == 3)
     def _():
         to_own[1].start()
-        to_own[2].start()
-
-    send(mine, 8 + y, slab + column[2]).start()
+
 
     @pl.when(y < 3)
     def _():
@@ -257,6 +255,10 @@
     @pl.when(q > 0)
     def _():
         arrived(OWN)
+
+    @pl.when(q == 3)
+    def _():
+        to_own[2].start()
 
     own_slot = jnp.where(q == 0, y, OWN)
     send(units.at[own_slot], OPP, (me + 64) % 128).start()

time: 36.9 us -> 36.8 us (level)
  no operation moved by 1% of the time
where the time goes in v4:
time: 36.8 us; the launch traced here: 36.5 us
  Pallas kernels  35.9 us (98%)
  between operations  0.64 us (2%)
    pallas_call x1, Pallas kernels, body(): pl.pallas_call(kernel, out_shape=[pltpu.VMEM((16, 64, 256), F32), pltpu.V...  34.9 us
    pallas_call x1, Pallas kernels, body(): pl.pallas_call(finish, out_shape=[jax.ShapeDtypeStruct((16, 64, 256), F32...  0.99 us

profile of v4, /device:TPU:4, one launch (start us, length us, event | category | flops | bytes accessed | tf_op | source)
XLA Modules:
  0.0 36.5 jit_solution(7021398414013666524)
XLA Ops:
  0.6 34.9 %shard_map.77 = (f32[16,64,256]{2,1,0:T(8,128)S(1)}, f32[64,64]{1,0:T(8,128)S(1)}) custom-call(bf16[32,1024]{1,0:T(8,128)(2,1)} %bitcast.4, s32[8,128]{1,0:T(8,128)} %bitcast.5, bf16[2,512,256]{2,1,0:T(8,128)(2,1)} %constant.8.clone.first_hbm, f32[2,256,128]{2,1,0:T(8,128)} %constant.9.clone.twiddle_hbm, bf16[2,1024,256]{2,1,0:T(8,128)(2,1)} %constant.10.clone.second_hbm, ...), custom_call_target="tpu_custom_call" | custom-call | tf_op jit(solution)/shard_map/pallas_call | solution.py:347
  35.5 1.0 %shard_map.78 = (f32[16,64,256]{2,1,0:T(8,128)}, f32[64,64]{1,0:T(8,128)}) custom-call(f32[16,64,256]{2,1,0:T(8,128)S(1)} %get-tuple-element.6.cross, f32[64,64]{1,0:T(8,128)S(1)} %get-tuple-element.7.opposite), custom_call_target="tpu_custom_call" | custom-call | tf_op jit(solution)/shard_map/pallas_call | solution.py:373

commit v5 on v4

--- a/solution.py
+++ b/solution.py
@@ -90,8 +90,8 @@
         greet(peer2((z + d) % 16), q - core)
     for d in range(1, 8):
         greet(peer1((spot + d) % 8), q - core + 1)
-    for blk in (up1, down1, up2, down2):
-        greet(blk + y, q - core)
+    for blk, wraps in ((up1, z == 15), (down1, z == 0), (up2, z >= 14), (down2, z <= 1)):
+        pl.when(wraps)(lambda blk=blk: greet(blk + y, q - core))
     for blk in (up1, down1):
         for k in (1, 3):
             greet(blk + column[k], q - core)
@@ -159,7 +159,7 @@
 
     @pl.when(core == 0)
     def _():
-        pl.semaphore_wait(barrier, 1 + 2 * (15 + 4 + 4) + jnp.where(q == 2, 1, 0))
+        pl.semaphore_wait(barrier, 1 + 2 * (15 + 4 + jnp.where(jnp.logical_or(z == 0, z == 15), 2, jnp.where(jnp.logical_or(z == 1, z == 14), 1, 0))) + jnp.where(q == 2, 1, 0))
         pl.semaphore_signal(far_sem, 1, device_id=device(me, other), device_id_type=MESH)
 
     for c in stage1:
@@ -236,9 +236,9 @@
         send(mine, 8 + y, slab + column[k]).start()
     send(mine, 4 + y, up1 + y).start()
     send(mine, 12 + y, down1 + y).start()
-    for k in (1, 3):
-        send(mine, 4 + y, up1 + column[k]).start()
-        send(mine, 12 + y, down1 + column[k]).start()
+    for first, blk in ((4, up1), (12, down1)):
+        for k in (1, 3):
+            send(mine, first + y, blk + column[k]).start()
 
     arrived(8 + column[2])
     send(units.at[8 + column[2]], 4 + column[2], up1 + y).start()

time: 36.8 us -> 36.8 us (level)
  the two profiles are of different devices: /device:TPU:4 before, /device:TPU:8 now
where the time goes in v5:
time: 36.8 us; the launch traced here: 36.6 us
  Pallas kernels  36 us (98%)
  between operations  0.64 us (2%)
    pallas_call x1, Pallas kernels, body(): pl.pallas_call(kernel, out_shape=[pltpu.VMEM((16, 64, 256), F32), pltpu.V...  35 us
    pallas_call x1, Pallas kernels, body(): pl.pallas_call(finish, out_shape=[jax.ShapeDtypeStruct((16, 64, 256), F32...  0.99 us

profile of v5, /device:TPU:8, one launch (start us, length us, event | category | flops | bytes accessed | tf_op | source)
XLA Modules:
  0.0 36.6 jit_solution(18116117213246766963)
XLA Ops:
  0.6 35.0 %shard_map.77 = (f32[16,64,256]{2,1,0:T(8,128)S(1)}, f32[64,64]{1,0:T(8,128)S(1)}) custom-call(bf16[32,1024]{1,0:T(8,128)(2,1)} %bitcast.4, s32[8,128]{1,0:T(8,128)} %bitcast.5, bf16[2,512,256]{2,1,0:T(8,128)(2,1)} %constant.8.clone.first_hbm, f32[2,256,128]{2,1,0:T(8,128)} %constant.9.clone.twiddle_hbm, bf16[2,1024,256]{2,1,0:T(8,128)(2,1)} %constant.10.clone.second_hbm, ...), custom_call_target="tpu_custom_call" | custom-call | tf_op jit(solution)/shard_map/pallas_call | solution.py:347
  35.7 1.0 %shard_map.78 = (f32[16,64,256]{2,1,0:T(8,128)}, f32[64,64]{1,0:T(8,128)}) custom-call(f32[16,64,256]{2,1,0:T(8,128)S(1)} %get-tuple-element.6.cross, f32[64,64]{1,0:T(8,128)S(1)} %get-tuple-element.7.opposite), custom_call_target="tpu_custom_call" | custom-call | tf_op jit(solution)/shard_map/pallas_call | solution.py:373

commit v6 on v4

--- a/solution.py
+++ b/solution.py
@@ -86,10 +86,10 @@
     up1, down1, up2, down2 = (slab + 4) % 128, (slab + 124) % 128, (slab + 8) % 128, (slab + 120) % 128
     column = {k: (y + k) % 4 for k in (1, 2, 3)}
     greet(me, other)
+    for d in range(1, 8):
+        greet(peer1((spot + d) % 8), q - core + 1)
     for d in (8, 7, 9, 6, 10, 5, 11, 4, 12, 3, 13, 2, 14, 1, 15):
         greet(peer2((z + d) % 16), q - core)
-    for d in range(1, 8):
-        greet(peer1((spot + d) % 8), q - core + 1)
     for blk in (up1, down1, up2, down2):
         greet(blk + y, q - core)
     for blk in (up1, down1):

time: 36.8 us -> 36.6 us (level)
  no operation moved by 1% of the time
where the time goes in v6:
time: 36.6 us; the launch traced here: 36.4 us
  Pallas kernels  35.8 us (98%)
  between operations  0.64 us (2%)
    pallas_call x1, Pallas kernels, body(): pl.pallas_call(kernel, out_shape=[pltpu.VMEM((16, 64, 256), F32), pltpu.V...  34.8 us
    pallas_call x1, Pallas kernels, body(): pl.pallas_call(finish, out_shape=[jax.ShapeDtypeStruct((16, 64, 256), F32...  0.99 us

profile of v6, /device:TPU:4, one launch (start us, length us, event | category | flops | bytes accessed | tf_op | source)
XLA Modules:
  0.0 36.4 jit_solution(7749369078525855237)
XLA Ops:
  0.6 34.8 %shard_map.77 = (f32[16,64,256]{2,1,0:T(8,128)S(1)}, f32[64,64]{1,0:T(8,128)S(1)}) custom-call(bf16[32,1024]{1,0:T(8,128)(2,1)} %bitcast.4, s32[8,128]{1,0:T(8,128)} %bitcast.5, bf16[2,512,256]{2,1,0:T(8,128)(2,1)} %constant.8.clone.first_hbm, f32[2,256,128]{2,1,0:T(8,128)} %constant.9.clone.twiddle_hbm, bf16[2,1024,256]{2,1,0:T(8,128)(2,1)} %constant.10.clone.second_hbm, ...), custom_call_target="tpu_custom_call" | custom-call | tf_op jit(solution)/shard_map/pallas_call | solution.py:347
  35.4 1.0 %shard_map.78 = (f32[16,64,256]{2,1,0:T(8,128)}, f32[64,64]{1,0:T(8,128)}) custom-call(f32[16,64,256]{2,1,0:T(8,128)S(1)} %get-tuple-element.6.cross, f32[64,64]{1,0:T(8,128)S(1)} %get-tuple-element.7.opposite), custom_call_target="tpu_custom_call" | custom-call | tf_op jit(solution)/shard_map/pallas_call | solution.py:373
